TPU v7x, 512 devices: a whole 4x4x16 slice. The times are simulated.
512 devices in a mesh: pair: 4 (over y_lo, core), slab: 128 (over x, z, y_hi).
Axes of the slice: x: 4, y: 4 (y_hi: 2, y_lo: 2; y = y_hi * 2 + y_lo), z: 16, core: 2. Of those that a mesh axis runs over, the one named last changes fastest.
Arguments:
- amplitudes: bfloat16 [512, 802816], P('pair', 'slab'), may hold values from -24 to 24
- integrals: bfloat16 [256, 802816], P('pair', 'slab'), may hold values from -0.0068359375 to 0.0068359375
- pair_list: int32 [512, 2], P('slab'), may hold values from 0 to 199, as said below
Outputs:
- residual: bfloat16 [512, 256], P('slab', 'pair')
Inputs may be any that keep to these rules, and one draw needn't show every extreme that they name: `pair_list`: each row is a packed pair (i, j) with i <= j; no pair appears twice; the pairs (0, 0) and (199, 199) are always present.
All inputs are finite; a program needn't handle non-finite values.
Results may differ from a plain program's by a relative error of at most 0.0051.
Values may be sent and summed in bfloat16 or wider, within the bound.
A program may use at most 128 MiB of HBM per device.

v0:
```python
import jax
import jax.numpy as jnp
from jax import lax
from jax.sharding import PartitionSpec as P

C_DEV = 7


def body(amplitudes, integrals, pair_list):
    groups = lax.axis_size("slab")
    width = amplitudes.shape[1]
    whole = lax.all_gather(amplitudes, "pair", axis=0, tiled=True)
    count = whole.shape[0]
    arrived = lax.all_to_all(
        whole.reshape(count, C_DEV, groups, C_DEV), "slab", split_axis=2, concat_axis=2, tiled=True
    )
    mirrored = jnp.swapaxes(arrived, 1, 3).reshape(count, width)
    symmetric = (whole.astype(jnp.float32) + mirrored.astype(jnp.float32)).astype(jnp.bfloat16)
    ladder = lax.psum_scatter(
        lax.dot_general(
            symmetric, integrals, (((1,), (1,)), ((), ())), preferred_element_type=jnp.float32
        ),
        "slab",
        scatter_dimension=0,
        tiled=True,
    )
    weight = jnp.where(pair_list[:, 0] == pair_list[:, 1], 0.5, 1.0).astype(jnp.float32)
    return (ladder * weight[:, None]).astype(jnp.bfloat16)


def solution(mesh):
    placed = (P("pair", "slab"), P("pair", "slab"), P("slab", None))
    return jax.shard_map(
        body, mesh=mesh, in_specs=placed, out_specs=P("slab", "pair"), check_vma=False
    )
```

profile of v0, /device:TPU:8, one launch (start us, length us, event | category | flops | bytes accessed | tf_op | source)
XLA Modules:
  0.0 1746.0 jit_solution(10554821379101877975)
XLA Ops:
  6.5 0.0 copy-start
  6.5 0.0 all-gather.2.cloned.1.call-start
  6.5 3.8 copy.7
  10.3 0.0 all-gather.2.cloned.1.call-update
  10.3 75.5 %all-gather.2.cloned.1.call-done = bf16[512,6272]{0,1:T(8,128)(2,1)} async-done(((bf16[128,6272]{0,1:T(8,128)(2,1)}), bf16[512,6272]{0,1:T(8,128)(2,1)}) %all-gather.2.cloned.1.call-update) | async-done | bytes 6422544 | tf_op jit(solution)/shard_map/all_gather | solution.py:12
  85.9 10.7 reshape.6
  96.6 6.5 copy.8
  103.1 18.8 %all-to-all-start = ((bf16[512,7,128,7]{0,3,1,2:T(8,128)(2,1)}), bf16[512,7,128,7]{0,3,1,2:T(8,128)(2,1)}, u32[]{:S(2)}, u32[]{:S(2)}) async-start(bf16[512,7,128,7]{0,3,1,2:T(8,128)(2,1)} %copy.8), calls=%async_computation | async-start | bytes 14680064 | tf_op jit(solution)/shard_map/all_to_all | solution.py:14
  121.9 0.2 all-reduce.3.cloned.1.call-start
  122.2 1.3 dynamic-slice
  124.1 320.1 %all-to-all-done = bf16[512,7,128,7]{0,3,1,2:T(8,128)(2,1)} async-done(((bf16[512,7,128,7]{0,3,1,2:T(8,128)(2,1)}), bf16[512,7,128,7]{0,3,1,2:T(8,128)(2,1)}, u32[]{:S(2)}, u32[]{:S(2)}) %all-to-all-start) | async-done | bytes 6422560 | tf_op jit(solution)/shard_map/all_to_all | solution.py:14
  444.2 10.4 convert_bitcast_fusion
  454.6 17.9 %copy.9 = f32[512,7,128,7]{0,3,2,1:T(8,128)} copy(f32[512,7,128,7]{0,1,3,2:T(8,128)} %convert_bitcast_fusion) | data formatting | bytes 25690112 | tf_op jit(solution)/shard_map/convert_element_type | solution.py:18
  472.5 14.9 reshape.7
  487.4 0.0 copy-done
  487.4 0.0 copy-start.1
  487.4 9.4 fusion
  496.8 0.0 all-reduce.3.cloned.1.call-update
  496.8 0.0 copy-done.1
  496.9 1241.0 %all-reduce.3.cloned.1.call-done = f32[512,64]{1,0:T(8,128)} async-done(((f32[512,64]{1,0:T(8,128)}), f32[512,64]{1,0:T(8,128)}) %all-reduce.3.cloned.1.call-update) | async-done | bytes 131088
  1737.9 1.3 fusion.1
  (1 shorter events, 0.0 us)
Async XLA Ops:
  6.5 480.9 %copy-start = (bf16[64,6272]{1,0:T(8,128)(2,1)S(1)}, bf16[64,6272]{1,0:T(8,128)(2,1)}, u32[]{:S(2)}) copy-start(bf16[64,6272]{1,0:T(8,128)(2,1)} %param.4) | copy-start | bytes 2408452
  6.5 79.3 %all-gather.2.cloned.1.call-start = ((), (), s32[]{:S(2)}) async-start(), calls=%async_computation.1 | async-start | bytes 8028160 | tf_op jit(solution)/shard_map/all_gather | solution.py:12
  103.1 341.1 %all-to-all-start = ((bf16[512,7,128,7]{0,3,1,2:T(8,128)(2,1)}), bf16[512,7,128,7]{0,3,1,2:T(8,128)(2,1)}, u32[]{:S(2)}, u32[]{:S(2)}) async-start(bf16[512,7,128,7]{0,3,1,2:T(8,128)(2,1)} %copy.8), calls=%async_computation | async-start | bytes 14680064 | tf_op jit(solution)/shard_map/all_to_all | solution.py:14
  121.9 1615.9 %all-reduce.3.cloned.1.call-start = ((), (), s32[]{:S(2)}) async-start(), calls=%async_computation.2 | async-start | bytes 524288
  487.4 9.4 copy-start.1
Sparse Core Ops, SparseCore 0:
  10.5 75.3 all-gather.1
  497.0 1240.8 all-reduce.2
where the time goes:
time: 1750 us
  waiting for transfers between devices  1640 us (94%)
  local copies, waits for them, and re-layouts  55 us (3%)
  starting transfers between devices  19.1 us (1%)
    unnamed x3, waiting for transfers between devices  1240 us
    all_to_all x1, waiting for transfers between devices, body(): lax.all_to_all(whole.reshape(count, C_DEV, groups, C_DEV), 'slab', split_...  320 us
    all_gather x1, waiting for transfers between devices, body(): whole = lax.all_gather(amplitudes, 'pair', axis=0, tiled=True)  75.5 us
  transfers between devices with their start and end apart: 3, of which 3 were waited for; matrix products, arithmetic and copies ran while one was open for 0% of the time, Pallas kernels for 0%

commit v1 on v0

v1 whole, which is shorter than its diff:
```python
import jax
import jax.numpy as jnp
from jax import lax
from jax.sharding import PartitionSpec as P

C_DEV = 7


def body(amplitudes, integrals, pair_list):
    groups = lax.axis_size("slab")
    rows, width = integrals.shape
    arrived = lax.all_to_all(
        integrals.reshape(rows, C_DEV, groups, C_DEV), "slab", split_axis=2, concat_axis=2, tiled=True
    )
    mirrored = jnp.swapaxes(arrived, 1, 3).reshape(rows, width)
    symmetric = (integrals.astype(jnp.float32) + mirrored.astype(jnp.float32)).astype(jnp.bfloat16)
    whole = lax.all_gather(symmetric, "pair", axis=0, tiled=True)
    part = lax.dot_general(
        amplitudes, whole, (((1,), (1,)), ((), ())), preferred_element_type=jnp.float32
    )
    part = lax.all_to_all(part, "pair", split_axis=1, concat_axis=0, tiled=True)
    terms = lax.all_to_all(
        part.reshape(groups, -1, part.shape[1]), "slab", split_axis=0, concat_axis=0, tiled=True
    )
    ladder = jnp.sum(terms, axis=0)
    weight = jnp.where(pair_list[:, 0] == pair_list[:, 1], 0.5, 1.0).astype(jnp.float32)
    return (ladder * weight[:, None]).astype(jnp.bfloat16)


def solution(mesh):
    placed = (P("pair", "slab"), P("pair", "slab"), P("slab", None))
    return jax.shard_map(
        body, mesh=mesh, in_specs=placed, out_specs=P("slab", "pair"), check_vma=False
    )
```

time: 1750 us -> 197 us (0.11)
  waiting for transfers between devices: 1640 us -> 55.7 us
  blocking collectives: 0 us -> 76 us
  local copies, waits for them, and re-layouts: 55 us -> 25.8 us
    unnamed x3 -> x1, waiting for transfers between devices: 1240 us -> 0.02 us
    all_to_all x1, waiting for transfers between devices: 320 us -> 19.7 us  [body(): lax.all_to_all(part.reshape(groups, -1, part.shape[1]), 'slab', split_axi...]
    all_to_all x0 -> x2, blocking collectives: none -> 76 us  [the longest x1 68.6 us: body(): lax.all_to_all(integrals.reshape(rows, C_DEV, groups, C_DEV), 'slab', spl...]
    all_gather x1, waiting for transfers between devices: 75.5 us -> 36 us  [body(): whole = lax.all_gather(symmetric, 'pair', axis=0, tiled=True)]
    convert_element_type x2 -> x3, local copies, waits for them, and re-layouts: 32.8 us -> 9.59 us  [body(): mirrored.astype(jnp.float32)]
  transfers between devices with their start and end apart: 3 -> 2, of which waited for: 3 -> 2; matrix products, arithmetic and copies ran while one was open for 0% -> 0% of each run, Pallas kernels for 0% -> 0%
where the time goes in v1:
time: 197 us; the launch traced here: 196 us
  blocking collectives  76 us (39%)
  waiting for transfers between devices  55.7 us (28%)
  local copies, waits for them, and re-layouts  25.8 us (13%)
  starting transfers between devices  18.4 us (9%)
  between operations  13.5 us (7%)
  other arithmetic  4.14 us (2%)
  matrix products  2.89 us (1%)
    all_to_all x1, blocking collectives, body(): lax.all_to_all(integrals.reshape(rows, C_DEV, groups, C_DEV), 'slab', spl...  68.6 us
    all_gather x1, waiting for transfers between devices, body(): whole = lax.all_gather(symmetric, 'pair', axis=0, tiled=True)  36 us
    all_to_all x1, waiting for transfers between devices, body(): lax.all_to_all(part.reshape(groups, -1, part.shape[1]), 'slab', split_axi...  19.7 us
    all_to_all x1, starting transfers between devices, body(): lax.all_to_all(part.reshape(groups, -1, part.shape[1]), 'slab', split_axi...  18.4 us
    unnamed x9, local copies, waits for them, and re-layouts  11.2 us
    convert_element_type x3, local copies, waits for them, and re-layouts, body(): mirrored.astype(jnp.float32)  9.59 us
    all_to_all x1, blocking collectives, body(): part = lax.all_to_all(part, 'pair', split_axis=1, concat_axis=0, tiled=True)  7.37 us
    reshape x2, local copies, waits for them, and re-layouts, body(): integrals.reshape(rows, C_DEV, groups, C_DEV)  4.28 us
  transfers between devices with their start and end apart: 2, of which 2 were waited for; matrix products, arithmetic and copies ran while one was open for 0% of the time, Pallas kernels for 0%

profile of v1, /device:TPU:8, one launch (start us, length us, event | category | flops | bytes accessed | tf_op | source)
XLA Modules:
  0.0 196.4 jit_solution(11130381142198263321)
XLA Ops:
  6.5 0.0 copy-start
  6.5 0.0 all-gather.2.cloned.1.call-start
  6.5 2.6 %copy.15 = bf16[64,6272]{0,1:T(8,128)(2,1)} copy(bf16[64,6272]{1,0:T(8,128)(2,1)} %param.4) | data formatting | bytes 1605632 | tf_op args[1]
  9.2 2.7 %reshape.13 = bf16[64,7,128,7]{0,3,2,1:T(8,128)(2,1)S(1)} reshape(bf16[64,6272]{0,1:T(8,128)(2,1)} %copy.15) | data formatting | bytes 1605632 | tf_op jit(solution)/shard_map/reshape | solution.py:13
  11.9 1.6 copy.21
  13.5 3.6 %reshape.16 = bf16[128,2,1568]{2,1,0:T(2,128)(2,1)S(1)} reshape(bf16[128,7,7,64]{3,2,1,0:T(8,128)(2,1)} %bitcast.20) | data formatting | bytes 1605632
  17.0 68.6 %all_to_all.26 = bf16[128,2,1568]{2,1,0:T(2,128)(2,1)} all-to-all(bf16[128,2,1568]{2,1,0:T(2,128)(2,1)S(1)} %reshape.16), channel_id=1, replica_groups=mesh['pair'=4,'slab'=128] {'slab'}, dimensions={0} | all-to-all | bytes 1605632 | tf_op jit(solution)/shard_map/all_to_all | solution.py:12
  85.7 4.0 %reshape.17 = bf16[128,7,7,64]{3,2,1,0:T(8,128)(2,1)S(1)} reshape(bf16[128,2,1568]{2,1,0:T(2,128)(2,1)} %all_to_all.26) | data formatting | bytes 1605632
  89.7 0.2 convert_bitcast_fusion
  89.9 2.4 %copy.17 = f32[64,7,128,7]{0,3,2,1:T(8,128)} copy(f32[64,7,128,7]{0,1,3,2:T(8,128)S(1)} %convert_bitcast_fusion) | data formatting | bytes 3211264 | tf_op jit(solution)/shard_map/convert_element_type | solution.py:16
  92.4 4.6 %reshape.15 = f32[64,6272]{0,1:T(8,128)} reshape(f32[64,7,128,7]{0,3,2,1:T(8,128)} %copy.17) | data formatting | bytes 3211264 | tf_op jit(solution)/shard_map/convert_element_type | solution.py:16
  97.0 2.6 %copy.18 = f32[64,6272]{1,0:T(8,128)S(1)} copy(f32[64,6272]{0,1:T(8,128)} %reshape.15) | data formatting | bytes 3211264 | tf_op jit(solution)/shard_map/convert_element_type | solution.py:16
  99.5 2.2 %add_convert_fusion = bf16[64,6272]{1,0:T(8,128)(2,1)} fusion(f32[64,6272]{1,0:T(8,128)S(1)} %copy.18, bf16[64,6272]{1,0:T(8,128)(2,1)} %param.4), kind=kLoop, calls=%fused_computation.1 | loop fusion | flops 1204224 | bytes 3211264 | tf_op jit(solution)/shard_map/convert_element_type | solution.py:16
  101.7 0.0 all-gather.2.cloned.1.call-update
  101.7 0.0 copy-start.1
  101.7 36.0 %all-gather.2.cloned.1.call-done = bf16[256,6272]{1,0:T(8,128)(2,1)} async-done(((bf16[64,6272]{1,0:T(8,128)(2,1)}), bf16[256,6272]{1,0:T(8,128)(2,1)}) %all-gather.2.cloned.1.call-update) | async-done | bytes 3211280 | tf_op jit(solution)/shard_map/all_gather | solution.py:17
  137.8 0.0 copy-done
  137.8 2.9 %fusion.1 = f32[256,128]{1,0:T(8,128)S(1)} fusion(bf16[256,6272]{1,0:T(8,128)(2,1)} %all-gather.2.cloned.1.call-done, bf16[128,6272]{1,0:T(8,128)(2,1)S(1)} %copy-done), kind=kOutput, calls=%fused_computation.6 | convolution fusion | flops 411041792 | bytes 4947968 | tf_op jit(solution)/shard_map/dot_general | solution.py:18
  140.7 7.4 %all_to_all.27 = f32[128,4,64]{0,2,1:T(8,128)S(1)} all-to-all(f32[128,4,64]{0,2,1:T(8,128)S(1)} %bitcast.22), channel_id=1, replica_groups=mesh['pair'=4,'slab'=128] {'pair'}, dimensions={1} | all-to-all | bytes 262144 | tf_op jit(solution)/shard_map/all_to_all | solution.py:21
  148.0 0.1 copy.19
  148.2 0.9 reshape.18
  149.1 18.4 %all-to-all-start.2 = ((f32[128,1,256]{2,1,0:T(1,128)}), f32[128,1,256]{2,1,0:T(1,128)S(1)}, u32[]{:S(2)}, u32[]{:S(2)}) async-start(f32[128,1,256]{2,1,0:T(1,128)} %reshape.18), calls=%async_computation.2 | async-start | bytes 262144 | tf_op jit(solution)/shard_map/all_to_all | solution.py:22
  167.4 0.0 copy-done.1
  167.5 19.7 %all-to-all-done.2 = f32[128,1,256]{2,1,0:T(1,128)S(1)} async-done(((f32[128,1,256]{2,1,0:T(1,128)}), f32[128,1,256]{2,1,0:T(1,128)S(1)}, u32[]{:S(2)}, u32[]{:S(2)}) %all-to-all-start.2) | async-done | bytes 131104 | tf_op jit(solution)/shard_map/all_to_all | solution.py:22
  187.1 0.5 broadcast.2
  187.6 1.0 reduce
  188.6 0.2 reshape.19
  188.8 0.1 reduce_sum.9
  188.9 0.6 multiply_convert_fusion
  (1 shorter events, 0.0 us)
Async XLA Ops:
  6.5 131.2 %copy-start = (bf16[128,6272]{1,0:T(8,128)(2,1)S(1)}, bf16[128,6272]{1,0:T(8,128)(2,1)}, u32[]{:S(2)}) copy-start(bf16[128,6272]{1,0:T(8,128)(2,1)} %param.3) | copy-start | bytes 4816900
  6.5 131.2 %all-gather.2.cloned.1.call-start = ((), (), s32[]{:S(2)}) async-start(), calls=%async_computation.3 | async-start | bytes 4014080 | tf_op jit(solution)/shard_map/all_gather | solution.py:17
  101.7 65.7 %copy-start.1 = (s32[4,2]{0,1:T(2,128)S(1)}, s32[4,2]{0,1:T(2,128)}, u32[]{:S(2)}) copy-start(s32[4,2]{0,1:T(2,128)} %param.5) | copy-start | bytes 100
  149.1 38.1 %all-to-all-start.2 = ((f32[128,1,256]{2,1,0:T(1,128)}), f32[128,1,256]{2,1,0:T(1,128)S(1)}, u32[]{:S(2)}, u32[]{:S(2)}) async-start(f32[128,1,256]{2,1,0:T(1,128)} %reshape.18), calls=%async_computation.2 | async-start | bytes 262144 | tf_op jit(solution)/shard_map/all_to_all | solution.py:22
Sparse Core Ops, SparseCore 0:
  101.8 35.8 all-gather.1

commit v2 on v1

v2 whole, which is shorter than its diff:
```python
import jax
import jax.numpy as jnp
from jax import lax
from jax.experimental import pallas as pl
from jax.experimental.pallas import tpu as pltpu
from jax.sharding import PartitionSpec as P

MESH = pl.DeviceIdType.MESH
NV = 896
C = 7
BF = jnp.bfloat16
F32 = jnp.float32


def dot(a, b):
    return jnp.dot(a, b, preferred_element_type=F32)


def dot_nt(a, b):
    return lax.dot_general(a, b, (((1,), (1,)), ((), ())), preferred_element_type=F32)


def iotas(rows, cols):
    return (
        lax.broadcasted_iota(jnp.int32, (rows, cols), 0),
        lax.broadcasted_iota(jnp.int32, (rows, cols), 1),
    )


def one_hot(hit):
    return jnp.where(hit, 1.0, 0.0).astype(BF)


def kernel(
    amp, ints, out,
    i_all, a_all, pick, pack, turn, spread, w, xin, zout, zin, sym, other, aq, acc, r1in, r1sum, r2in,
    load, swap_s, swap_r, xy_s, xy_r, z_s, z_r, lo_s, lo_r, r1_s, r1_r, r2_s, r2_r,
):
    q, s = lax.axis_index("pair"), lax.axis_index("slab")
    l, k = q // 2, q % 2
    x, z, y = s // 32, (s // 2) % 16, s % 2
    me = x * 2 + y
    parity = (z + k) % 2

    def slab(xx, zz, yy):
        return (xx * 16 + zz) * 2 + yy

    def offset(t):
        half = t + 1 - parity
        return (8 - parity - 2 * (half // 2)) * (1 - 2 * (half % 2))

    def goes_to(t):
        return (z + offset(t) + 16) % 16

    def comes_from(t):
        return (z - offset(t) + 16) % 16

    def z_peer(t):
        return (l * 2 + z % 2, slab(x, goes_to(t), y))

    sibling = (l * 2 + 1 - k, s)
    across = ((1 - l) * 2 + k, s)
    near = [((x + a) % 4, (y + b) % 2) for a in range(4) for b in range(2) if a or b]

    barrier = pltpu.get_barrier_semaphore()

    def greet(device):
        pl.semaphore_signal(barrier, inc=1, device_id=device, device_id_type=MESH)

    greet(sibling)
    greet(across)
    for xx, yy in near:
        greet((q, slab(xx, z, yy)))
    for t in range(7):
        greet(z_peer(t))

    @pl.when(parity == 1)
    def _():
        greet(z_peer(7))

    load_i = pltpu.make_async_copy(ints, i_all.at[k], load.at[0])
    load_a = pltpu.make_async_copy(amp, a_all.at[k], load.at[1])
    load_i.start()
    load_a.start()

    r, c = iotas(512, NV)
    m, delta = (r >> 3) & 7, r & 7
    d = 224 * (m >> 1) + 28 * (r >> 6) + 14 * k + 7 * (m & 1) + delta
    pick[...] = one_hot((c == d) & (delta < 7))
    r, c = iotas(400, 512)
    i, j = (c >> 3) & 7, c & 7
    pack[...] = one_hot((r == (c >> 6) * 49 + i * 7 + j) & (i < 7) & (j < 7))
    r, c = iotas(448, 400)
    i = r & 7
    turn[...] = one_hot((c == ((r >> 3) & 7) * 49 + i * 7 + (r >> 6)) & (i < 7))

    def make_spread(g, carry):
        r, c = iotas(NV, 256)
        m, delta = (c >> 3) & 7, c & 7
        d = 224 * (m >> 1) + 28 * (2 * g + (c >> 7)) + 14 * k + 7 * (m & 1) + delta
        hit = (r == d) & (delta < 7)
        upper = ((c >> 6) & 1) == 1
        spread[0, g] = one_hot(hit & ~upper)
        spread[1, g] = one_hot(hit & upper)
        return carry

    lax.fori_loop(0, 4, make_spread, 0)

    load_i.wait()
    load_a.wait()

    @pl.when(parity == 1)
    def _():
        pl.semaphore_wait(barrier, 17)

    @pl.when(parity == 0)
    def _():
        pl.semaphore_wait(barrier, 16)

    def swap(ref, n):
        return pltpu.make_async_remote_copy(
            src_ref=ref.at[k], dst_ref=ref.at[k], send_sem=swap_s.at[n], recv_sem=swap_r.at[n],
            device_id=sibling, device_id_type=MESH,
        )

    def swap_in(ref, n):
        return pltpu.make_async_remote_copy(
            src_ref=ref.at[1 - k], dst_ref=ref.at[1 - k], send_sem=swap_s.at[n], recv_sem=swap_r.at[n],
            device_id=sibling, device_id_type=MESH,
        )

    swap(i_all, 0).start()
    swap_in(i_all, 0).wait_recv()
    swap(a_all, 1).start()

    def rows_of(c):
        return dot_nt(pick[...], i_all[:, :, c * NV:(c + 1) * NV].reshape(128, NV)).reshape(64, 8, 128)

    for a in range(4):
        low = rows_of(2 * a)
        high = rows_of(2 * a + 1) if a < 3 else jnp.zeros_like(low)
        w[:, 16 * a:16 * a + 16, :] = jnp.stack([low, high], axis=1).reshape(64, 16, 128).astype(BF)

    def xy_copy(t, n):
        xx, yy = near[n]
        return pltpu.make_async_remote_copy(
            src_ref=w.at[(goes_to(t) // 2) * 8 + xx * 2 + yy], dst_ref=xin.at[t, me],
            send_sem=xy_s.at[t, n], recv_sem=xy_r.at[t, me],
            device_id=(q, slab(xx, z, yy)), device_id_type=MESH,
        )

    def xy_arrival(t, n):
        xx, yy = near[n]
        there = xx * 2 + yy
        return pltpu.make_async_remote_copy(
            src_ref=xin.at[t, there], dst_ref=xin.at[t, there],
            send_sem=xy_s.at[t, n], recv_sem=xy_r.at[t, there],
            device_id=(q, slab(xx, z, yy)), device_id_type=MESH,
        )

    def send_xy(t, carry):
        for n in range(7):
            xy_copy(t, n).start()
        return carry

    lax.fori_loop(0, 8, send_xy, 0)

    def z_copy(t):
        return pltpu.make_async_remote_copy(
            src_ref=zout.at[t], dst_ref=zin.at[t], send_sem=z_s.at[t], recv_sem=z_r.at[t],
            device_id=z_peer(t), device_id_type=MESH,
        )

    def relay(t, carry):
        xin[t, me] = w[(goes_to(t) // 2) * 8 + me]
        for n in range(7):
            xy_arrival(t, n).wait_recv()
        packed = dot(pack[...], xin[t].reshape(512, 128)).astype(BF)
        stays = offset(t) == 0

        @pl.when(stays)
        def _():
            zin[t] = packed

        @pl.when(jnp.logical_not(stays))
        def _():
            zout[t] = packed
            z_copy(t).start()

        return carry

    lax.fori_loop(0, 8, relay, 0)

    swap_in(a_all, 1).wait_recv()

    def order_amplitudes(g, carry):
        for a in range(4):
            c = 2 * a
            part = dot(a_all[:, :, c * NV:(c + 1) * NV].reshape(256, NV), spread[0, g])
            if a < 3:
                part += dot(a_all[:, :, (c + 1) * NV:(c + 2) * NV].reshape(256, NV), spread[1, g])
            part = part.astype(BF)
            aq[2 * g, :, 128 * a:128 * a + 128] = part[:, :128]
            aq[2 * g + 1, :, 128 * a:128 * a + 128] = part[:, 128:]
        return carry

    lax.fori_loop(0, 4, order_amplitudes, 0)

    acc[...] = jnp.zeros_like(acc)

    def lo_copy(t):
        return pltpu.make_async_remote_copy(
            src_ref=sym.at[t], dst_ref=other.at[t], send_sem=lo_s.at[t], recv_sem=lo_r.at[t],
            device_id=across, device_id_type=MESH,
        )

    def add_other(t):
        lo_copy(t).wait_recv()
        acc[1] += dot(aq[comes_from(t) // 2, :, :448], other[t])

    def symmetrize(t, carry):
        @pl.when(offset(t) != 0)
        def _():
            z_copy(t).wait_recv()

        zeta = comes_from(t) // 2
        mine = w[pl.ds(zeta * 8, 8)].astype(F32).reshape(8, 8, 8, 128)
        mine = jnp.concatenate([mine[:, c].reshape(64, 128) for c in range(C)], axis=0)
        sym[t] = (dot(turn[...], zin[t]) + mine).astype(BF)
        lo_copy(t).start()
        acc[0] += dot(aq[zeta, :, :448], sym[t])

        @pl.when(t > 0)
        def _():
            add_other(t - 1)

        return carry

    lax.fori_loop(0, 8, symmetrize, 0)
    add_other(7)

    mine16 = k * 8 + me

    def r1_copy(n):
        kk, xx, yy = n // 8, (n // 2) % 4, n % 2
        side = jnp.where(yy == l, 0, 1)
        return pltpu.make_async_remote_copy(
            src_ref=acc.at[side, pl.ds(pl.multiple_of(kk * 128 + xx * 32, 32), 32)], dst_ref=r1in.at[mine16],
            send_sem=r1_s.at[n], recv_sem=r1_r.at[mine16],
            device_id=(l * 2 + kk, slab(xx, z, yy)), device_id_type=MESH,
        )

    def r1_arrival(n):
        kk, xx, yy = n // 8, (n // 2) % 4, n % 2
        return pltpu.make_async_remote_copy(
            src_ref=r1in.at[n], dst_ref=r1in.at[n], send_sem=r1_s.at[n], recv_sem=r1_r.at[n],
            device_id=(l * 2 + kk, slab(xx, z, yy)), device_id_type=MESH,
        )

    def r1_send(n, carry):
        @pl.when(n != mine16)
        def _():
            r1_copy(n).start()

        return carry

    lax.fori_loop(0, 16, r1_send, 0)
    total = acc[jnp.where(y == l, 0, 1), pl.ds(pl.multiple_of(k * 128 + x * 32, 32), 32)]
    r1in[mine16] = total

    def r1_wait(n, carry):
        @pl.when(n != mine16)
        def _():
            r1_arrival(n).wait_recv()

        return carry

    lax.fori_loop(0, 16, r1_wait, 0)
    r1sum[...] = jnp.sum(r1in[...], axis=0).reshape(4, 8, 128)

    def r2_owner(n):
        u, yy, cc = n // 4, (n // 2) % 2, n % 2
        return 2 * y + cc, slab(q, 4 * x + u, yy)

    def r2_send(n, carry):
        u = n // 4
        qq, ss = r2_owner(n)
        here = (qq == q) & (ss == s)

        @pl.when(here)
        def _():
            r2in[z] = r1sum[u]

        @pl.when(jnp.logical_not(here))
        def _():
            pltpu.make_async_remote_copy(
                src_ref=r1sum.at[u], dst_ref=r2in.at[z], send_sem=r2_s.at[n], recv_sem=r2_r.at[z],
                device_id=(qq, ss), device_id_type=MESH,
            ).start()

        return carry

    lax.fori_loop(0, 16, r2_send, 0)

    def r2_wait(n, carry):
        qq, ss = x, slab(z // 4, n, q // 2)

        @pl.when(jnp.logical_not((qq == q) & (ss == s)))
        def _():
            pltpu.make_async_remote_copy(
                src_ref=r2in.at[n], dst_ref=r2in.at[n], send_sem=r2_s.at[n], recv_sem=r2_r.at[n],
                device_id=(qq, ss), device_id_type=MESH,
            ).wait_recv()

        return carry

    lax.fori_loop(0, 16, r2_wait, 0)
    done = jnp.sum(r2in[...], axis=0)
    done = jnp.where(y == 0, done[:4], done[4:])
    out[...] = jnp.where(k == 0, done[:, :64], done[:, 64:])

    swap(i_all, 0).wait_send()
    swap(a_all, 1).wait_send()

    def drain(t, carry):
        for n in range(7):
            xy_copy(t, n).wait_send()

        @pl.when(offset(t) != 0)
        def _():
            z_copy(t).wait_send()

        lo_copy(t).wait_send()
        return carry

    lax.fori_loop(0, 8, drain, 0)

    def drain_sums(n, carry):
        @pl.when(n != mine16)
        def _():
            r1_copy(n).wait_send()

        qq, ss = r2_owner(n)

        @pl.when(jnp.logical_not((qq == q) & (ss == s)))
        def _():
            pltpu.make_async_remote_copy(
                src_ref=r1sum.at[n // 4], dst_ref=r2in.at[z], send_sem=r2_s.at[n], recv_sem=r2_r.at[z],
                device_id=(qq, ss), device_id_type=MESH,
            ).wait_send()

        return carry

    lax.fori_loop(0, 16, drain_sums, 0)


def ladder_sum(amplitudes, integrals):
    dma = pltpu.SemaphoreType.DMA
    return pl.pallas_call(
        kernel,
        out_shape=jax.ShapeDtypeStruct((4, 64), F32),
        in_specs=[pl.BlockSpec(memory_space=pl.ANY)] * 2,
        out_specs=pl.BlockSpec(memory_space=pltpu.VMEM),
        scratch_shapes=[
            pltpu.VMEM((2, 64, C * NV), BF),
            pltpu.VMEM((2, 128, C * NV), BF),
            pltpu.VMEM((512, NV), BF),
            pltpu.VMEM((400, 512), BF),
            pltpu.VMEM((448, 400), BF),
            pltpu.VMEM((2, 4, NV, 256), BF),
            pltpu.VMEM((64, 64, 128), BF),
            pltpu.VMEM((8, 8, 64, 128), BF),
            pltpu.VMEM((8, 400, 128), BF),
            pltpu.VMEM((8, 400, 128), BF),
            pltpu.VMEM((8, 448, 128), BF),
            pltpu.VMEM((8, 448, 128), BF),
            pltpu.VMEM((8, 256, 512), BF),
            pltpu.VMEM((2, 256, 128), F32),
            pltpu.VMEM((16, 32, 128), F32),
            pltpu.VMEM((4, 8, 128), F32),
            pltpu.VMEM((16, 8, 128), F32),
            dma((2,)), dma((2,)), dma((2,)), dma((8, 8)), dma((8, 8)), dma((8,)), dma((8,)), dma((8,)), dma((8,)),
            dma((16,)), dma((16,)), dma((16,)), dma((16,)),
        ],
        compiler_params=pltpu.CompilerParams(
            collective_id=0, has_side_effects=True, vmem_limit_bytes=48 * 1024 * 1024
        ),
        cost_estimate=pl.CostEstimate(flops=4 * 10**9, bytes_accessed=2 * 10**7, transcendentals=0),
        name="ladder_sum",
    )(amplitudes, integrals)


def body(amplitudes, integrals, pair_list):
    ladder = ladder_sum(amplitudes, integrals)
    weight = jnp.where(pair_list[:, 0] == pair_list[:, 1], 0.5, 1.0).astype(jnp.float32)
    return (ladder * weight[:, None]).astype(BF)


def solution(mesh):
    placed = (P("pair", "slab"), P("pair", "slab"), P("slab", None))
    return jax.shard_map(
        body, mesh=mesh, in_specs=placed, out_specs=P("slab", "pair"), check_vma=False
    )
```

time: 197 us -> 98.8 us (0.50)
  the two profiles are of different devices: /device:TPU:8 before, /device:TPU:15 now
where the time goes in v2:
time: 98.8 us; the launch traced here: 98.6 us
  Pallas kernels  94.6 us (96%)
  local copies, waits for them, and re-layouts  2.56 us (3%)
  other arithmetic  1.39 us (1%)
    pallas_call x1, Pallas kernels, ladder_sum(): pl.pallas_call(kernel, out_shape=jax.ShapeDtypeStruct((4, 64), F32), in_s...  94.6 us
    unnamed x4, local copies, waits for them, and re-layouts  2.56 us

profile of v2, /device:TPU:15, one launch (start us, length us, event | category | flops | bytes accessed | tf_op | source)
XLA Modules:
  0.0 98.6 jit_solution(18032473025601204317)
XLA Ops:
  0.0 0.8 fusion
  0.8 0.0 copy-start
  0.8 1.4 %copy-done = bf16[128,6272]{1,0:T(8,128)(2,1)S(1)} copy-done((bf16[128,6272]{1,0:T(8,128)(2,1)S(1)}, bf16[128,6272]{1,0:T(8,128)(2,1)}, u32[]{:S(2)}) %copy-start) | copy-done | bytes 1605656
  2.2 0.0 copy-start.1
  2.2 1.1 %copy-done.1 = bf16[64,6272]{1,0:T(8,128)(2,1)S(1)} copy-done((bf16[64,6272]{1,0:T(8,128)(2,1)S(1)}, bf16[64,6272]{1,0:T(8,128)(2,1)}, u32[]{:S(2)}) %copy-start.1) | copy-done | bytes 802840
  3.3 94.6 %ladder_sum.1 = f32[4,64]{1,0:T(4,128)S(1)} custom-call(bf16[128,6272]{1,0:T(8,128)(2,1)S(1)} %copy-done, bf16[64,6272]{1,0:T(8,128)(2,1)S(1)} %copy-done.1), custom_call_target="tpu_custom_call" | custom-call | flops 4000000000 | bytes 20000000 | tf_op jit(solution)/shard_map/ladder_sum/pallas_call | solution.py:359
  97.9 0.6 multiply_convert_fusion
Async XLA Ops:
  0.8 1.4 %copy-start = (bf16[128,6272]{1,0:T(8,128)(2,1)S(1)}, bf16[128,6272]{1,0:T(8,128)(2,1)}, u32[]{:S(2)}) copy-start(bf16[128,6272]{1,0:T(8,128)(2,1)} %amp.1) | copy-start | bytes 4816900
  2.2 1.1 %copy-start.1 = (bf16[64,6272]{1,0:T(8,128)(2,1)S(1)}, bf16[64,6272]{1,0:T(8,128)(2,1)}, u32[]{:S(2)}) copy-start(bf16[64,6272]{1,0:T(8,128)(2,1)} %ints.1) | copy-start | bytes 2408452

commit v3 on v2

v3 whole, which is shorter than its diff:
```python
import jax
import jax.numpy as jnp
from jax import lax
from jax.experimental import pallas as pl
from jax.experimental.pallas import tpu as pltpu
from jax.sharding import PartitionSpec as P

MESH = pl.DeviceIdType.MESH
NV = 896
C = 7
BF = jnp.bfloat16
F32 = jnp.float32
SEND = (3, 2, 4, 1, 5, 0, 6, 7)
TAKE = (3, 2, 1, 4, 0, 5, 6, 7)


def entry(table, t):
    value = jnp.int32(table[0])
    for n in range(1, len(table)):
        value = jnp.where(t == n, table[n], value)
    return value


def dot(a, b):
    return jnp.dot(a, b, preferred_element_type=F32)


def dot_nt(a, b):
    return lax.dot_general(a, b, (((1,), (1,)), ((), ())), preferred_element_type=F32)


def iotas(rows, cols):
    return (
        lax.broadcasted_iota(jnp.int32, (rows, cols), 0),
        lax.broadcasted_iota(jnp.int32, (rows, cols), 1),
    )


def one_hot(hit):
    return jnp.where(hit, 1.0, 0.0).astype(BF)


def kernel(
    amp, ints, pairs, out,
    i_all, a_all, pick, pack, turn, spread, w, xin, zout, zin, sym, other, aq, acc, r1in, r1sum, r2in, ij,
    load, swap_s, swap_r, xy_s, xy_r, z_s, z_r, lo_s, lo_r, r1_s, r1_r, r2_s, r2_r,
):
    q, s = lax.axis_index("pair"), lax.axis_index("slab")
    l, k = q // 2, q % 2
    x, z, y = s // 32, (s // 2) % 16, s % 2
    me = x * 2 + y
    parity = (z + k) % 2

    def slab(xx, zz, yy):
        return (xx * 16 + zz) * 2 + yy

    def offset(t):
        half = 8 - t - parity
        return (8 - parity - 2 * (half // 2)) * (1 - 2 * (half % 2))

    def goes_to(t):
        return (z + offset(t) + 16) % 16

    def comes_from(t):
        return (z - offset(t) + 16) % 16

    def z_peer(t):
        return (l * 2 + z % 2, slab(x, goes_to(t), y))

    sibling = (l * 2 + 1 - k, s)
    across = ((1 - l) * 2 + k, s)
    steps = [(a, b) for a in range(4) for b in range(2) if a or b]
    near = [((x + a) % 4, (y + b) % 2) for a, b in steps]
    back = [steps.index(((4 - a) % 4, b)) for a, b in steps]

    barrier = pltpu.get_barrier_semaphore()

    def greet(device):
        pl.semaphore_signal(barrier, inc=1, device_id=device, device_id_type=MESH)

    greet(sibling)
    greet(across)
    for xx, yy in near:
        greet((q, slab(xx, z, yy)))
    for t in range(1, 8):
        greet(z_peer(t))

    @pl.when(parity == 1)
    def _():
        greet(z_peer(0))

    load_i = pltpu.make_async_copy(ints, i_all.at[k], load.at[0])
    load_a = pltpu.make_async_copy(amp, a_all.at[k], load.at[1])
    load_i.start()
    load_a.start()
    load_p = pltpu.make_async_copy(pairs, ij, load.at[2])
    load_p.start()

    r, c = iotas(512, NV)
    m, delta = (r >> 3) & 7, r & 7
    d = 224 * (m >> 1) + 28 * (r >> 6) + 14 * k + 7 * (m & 1) + delta
    pick[...] = one_hot((c == d) & (delta < 7))

    load_i.wait()

    @pl.when(parity == 1)
    def _():
        pl.semaphore_wait(barrier, 17)

    @pl.when(parity == 0)
    def _():
        pl.semaphore_wait(barrier, 16)

    def swap(ref, n):
        return pltpu.make_async_remote_copy(
            src_ref=ref, dst_ref=ref, send_sem=swap_s.at[n], recv_sem=swap_r.at[n],
            device_id=sibling, device_id_type=MESH,
        )

    def part(core, a):
        return i_all.at[core, :, pl.ds(2 * a * NV, NV if a == 3 else 2 * NV)]

    for a in range(4):
        swap(part(k, a), a).start()

    def rows_of(c):
        return dot_nt(pick[...], i_all[:, :, c * NV:(c + 1) * NV].reshape(128, NV)).reshape(64, 8, 128)

    for a in range(4):
        swap(part(1 - k, a), a).wait_recv()
        low = rows_of(2 * a)
        high = rows_of(2 * a + 1) if a < 3 else jnp.zeros_like(low)
        w[:, 16 * a:16 * a + 16, :] = jnp.stack([low, high], axis=1).reshape(64, 16, 128).astype(BF)

    def xy_copy(t, n):
        xx, yy = near[n]
        return pltpu.make_async_remote_copy(
            src_ref=w.at[(goes_to(t) // 2) * 8 + xx * 2 + yy], dst_ref=xin.at[t, back[n]],
            send_sem=xy_s.at[t, n], recv_sem=xy_r.at[t, back[n]],
            device_id=(q, slab(xx, z, yy)), device_id_type=MESH,
        )

    def xy_arrival(t, n):
        xx, yy = near[n]
        return pltpu.make_async_remote_copy(
            src_ref=xin.at[t, n], dst_ref=xin.at[t, n],
            send_sem=xy_s.at[t, n], recv_sem=xy_r.at[t, n],
            device_id=(q, slab(xx, z, yy)), device_id_type=MESH,
        )

    def send_xy(t, carry):
        t = entry(SEND, t)
        for n in range(7):
            xy_copy(t, n).start()
        return carry


    def own_copy(t):
        return pltpu.make_async_remote_copy(
            src_ref=w.at[(goes_to(t) // 2) * 8 + me], dst_ref=zin.at[t, pl.ds(0, 64)],
            send_sem=z_s.at[0, t], recv_sem=z_r.at[0, t], device_id=z_peer(t), device_id_type=MESH,
        )

    def z_copy(t):
        return pltpu.make_async_remote_copy(
            src_ref=zout.at[t], dst_ref=zin.at[t, pl.ds(64, 352)],
            send_sem=z_s.at[1, t], recv_sem=z_r.at[1, t], device_id=z_peer(t), device_id_type=MESH,
        )

    def send_own(t, carry):
        t = entry(SEND, t)
        stays = offset(t) == 0

        @pl.when(stays)
        def _():
            zin[t, pl.ds(0, 64)] = w[(goes_to(t) // 2) * 8 + me]

        @pl.when(jnp.logical_not(stays))
        def _():
            own_copy(t).start()

        return carry

    lax.fori_loop(0, 8, send_own, 0)
    lax.fori_loop(0, 8, send_xy, 0)
    load_a.wait()
    load_p.wait()
    swap(a_all.at[k], 4).start()

    r, c = iotas(352, 448)
    i, j = (c >> 3) & 7, c & 7
    pack[...] = one_hot((r == (c >> 6) * 49 + i * 7 + j) & (i < 7) & (j < 7))

    def relay(t, carry):
        t = entry(SEND, t)
        for n in range(7):
            xy_arrival(t, n).wait_recv()
        packed = dot(pack[...], xin[t].reshape(448, 128)).astype(BF)
        stays = offset(t) == 0

        @pl.when(stays)
        def _():
            zin[t, pl.ds(64, 352)] = packed

        @pl.when(jnp.logical_not(stays))
        def _():
            zout[t] = packed
            z_copy(t).start()

        return carry

    lax.fori_loop(0, 8, relay, 0)

    def make_spread(g, carry):
        r, c = iotas(NV, 256)
        m, delta = (c >> 3) & 7, c & 7
        d = 224 * (m >> 1) + 28 * (2 * g + (c >> 7)) + 14 * k + 7 * (m & 1) + delta
        hit = (r == d) & (delta < 7)
        upper = ((c >> 6) & 1) == 1
        spread[0, g] = one_hot(hit & ~upper)
        spread[1, g] = one_hot(hit & upper)
        return carry

    lax.fori_loop(0, 4, make_spread, 0)

    r, c = iotas(448, 416)
    i, j, m = r & 7, r >> 6, (r >> 3) & 7
    n = (((m >> 1) - x) & 3) * 2 + (((m & 1) - y) & 1)
    turn[...] = one_hot((c == jnp.where(n == 0, i * 8 + j, 15 + n * 49 + i * 7 + j)) & (i < 7))

    swap(a_all.at[1 - k], 4).wait_recv()

    def order_amplitudes(g, carry):
        for a in range(4):
            c = 2 * a
            part = dot(a_all[:, :, c * NV:(c + 1) * NV].reshape(256, NV), spread[0, g])
            if a < 3:
                part += dot(a_all[:, :, (c + 1) * NV:(c + 2) * NV].reshape(256, NV), spread[1, g])
            part = part.astype(BF)
            aq[2 * g, :, 128 * a:128 * a + 128] = part[:, :128]
            aq[2 * g + 1, :, 128 * a:128 * a + 128] = part[:, 128:]
        return carry

    lax.fori_loop(0, 4, order_amplitudes, 0)

    acc[...] = jnp.zeros_like(acc)

    def lo_copy(t):
        return pltpu.make_async_remote_copy(
            src_ref=sym.at[t], dst_ref=other.at[t], send_sem=lo_s.at[t], recv_sem=lo_r.at[t],
            device_id=across, device_id_type=MESH,
        )

    def add_other(t):
        lo_copy(t).wait_recv()
        acc[1] += dot(aq[comes_from(t) // 2, :, :448], other[t])

    def symmetrize(step, carry):
        t = entry(TAKE, step)

        @pl.when(offset(t) != 0)
        def _():
            own_copy(t).wait_recv()
            z_copy(t).wait_recv()

        zeta = comes_from(t) // 2
        mine = w[pl.ds(zeta * 8, 8)].astype(F32).reshape(8, 8, 8, 128)
        mine = jnp.concatenate([mine[:, c].reshape(64, 128) for c in range(C)], axis=0)
        sym[t] = (dot(turn[...], zin[t]) + mine).astype(BF)
        lo_copy(t).start()
        acc[0] += dot(aq[zeta, :, :448], sym[t])

        @pl.when(step > 0)
        def _():
            add_other(entry(TAKE, step - 1))

        return carry

    lax.fori_loop(0, 8, symmetrize, 0)
    add_other(TAKE[7])

    mine16 = k * 8 + me

    def r1_copy(n):
        kk, xx, yy = n // 8, (n // 2) % 4, n % 2
        side = jnp.where(yy == l, 0, 1)
        return pltpu.make_async_remote_copy(
            src_ref=acc.at[side, pl.ds(pl.multiple_of(kk * 128 + xx * 32, 32), 32)], dst_ref=r1in.at[mine16],
            send_sem=r1_s.at[n], recv_sem=r1_r.at[mine16],
            device_id=(l * 2 + kk, slab(xx, z, yy)), device_id_type=MESH,
        )

    def r1_arrival(n):
        kk, xx, yy = n // 8, (n // 2) % 4, n % 2
        return pltpu.make_async_remote_copy(
            src_ref=r1in.at[n], dst_ref=r1in.at[n], send_sem=r1_s.at[n], recv_sem=r1_r.at[n],
            device_id=(l * 2 + kk, slab(xx, z, yy)), device_id_type=MESH,
        )

    def r1_send(n, carry):
        @pl.when(n != mine16)
        def _():
            r1_copy(n).start()

        return carry

    lax.fori_loop(0, 16, r1_send, 0)
    total = acc[jnp.where(y == l, 0, 1), pl.ds(pl.multiple_of(k * 128 + x * 32, 32), 32)]
    r1in[mine16] = total

    for a in range(4):
        swap(part(k, a), a).wait_send()
    swap(a_all.at[k], 4).wait_send()

    def drain(t, carry):
        for n in range(7):
            xy_copy(t, n).wait_send()

        @pl.when(offset(t) != 0)
        def _():
            own_copy(t).wait_send()
            z_copy(t).wait_send()

        lo_copy(t).wait_send()
        return carry

    lax.fori_loop(0, 8, drain, 0)

    def r1_wait(n, carry):
        @pl.when(n != mine16)
        def _():
            r1_arrival(n).wait_recv()

        return carry

    lax.fori_loop(0, 16, r1_wait, 0)
    r1sum[...] = jnp.sum(r1in[...], axis=0).reshape(4, 8, 128)

    def r2_owner(n):
        u, yy, cc = n // 4, (n // 2) % 2, n % 2
        return 2 * y + cc, slab(q, 4 * x + u, yy)

    def r2_copy(n):
        qq, ss = r2_owner(n)
        return pltpu.make_async_remote_copy(
            src_ref=r1sum.at[n // 4], dst_ref=r2in.at[z], send_sem=r2_s.at[n], recv_sem=r2_r.at[z],
            device_id=(qq, ss), device_id_type=MESH,
        )

    def r2_send(n, carry):
        u = n // 4
        qq, ss = r2_owner(n)
        here = (qq == q) & (ss == s)

        @pl.when(here)
        def _():
            r2in[z] = r1sum[u]

        @pl.when(jnp.logical_not(here))
        def _():
            r2_copy(n).start()

        return carry

    lax.fori_loop(0, 16, r2_send, 0)

    def drain_sums(n, carry):
        @pl.when(n != mine16)
        def _():
            r1_copy(n).wait_send()

        return carry

    lax.fori_loop(0, 16, drain_sums, 0)

    def r2_wait(n, carry):
        qq, ss = x, slab(z // 4, n, q // 2)

        @pl.when(jnp.logical_not((qq == q) & (ss == s)))
        def _():
            pltpu.make_async_remote_copy(
                src_ref=r2in.at[n], dst_ref=r2in.at[n], send_sem=r2_s.at[n], recv_sem=r2_r.at[n],
                device_id=(qq, ss), device_id_type=MESH,
            ).wait_recv()

        return carry

    lax.fori_loop(0, 16, r2_wait, 0)
    done = jnp.sum(r2in[...], axis=0)
    done = jnp.where(y == 0, done[:4], done[4:])
    done = jnp.where(k == 0, done[:, :64], done[:, 64:])
    weight = jnp.where(ij[0:1] == ij[1:2], 0.5, 1.0)
    r, c = iotas(4, 4)
    weight = jnp.sum(jnp.where(r == c, weight, 0.0), axis=1, keepdims=True)
    out[...] = done * weight

    def drain_tiles(n, carry):
        qq, ss = r2_owner(n)

        @pl.when(jnp.logical_not((qq == q) & (ss == s)))
        def _():
            r2_copy(n).wait_send()

        return carry

    lax.fori_loop(0, 16, drain_tiles, 0)


def ladder_sum(amplitudes, integrals, pair_list):
    dma = pltpu.SemaphoreType.DMA
    return pl.pallas_call(
        kernel,
        out_shape=jax.ShapeDtypeStruct((4, 64), F32),
        in_specs=[pl.BlockSpec(memory_space=pltpu.HBM)] * 3,
        out_specs=pl.BlockSpec(memory_space=pltpu.VMEM),
        scratch_shapes=[
            pltpu.VMEM((2, 64, C * NV), BF),
            pltpu.VMEM((2, 128, C * NV), BF),
            pltpu.VMEM((512, NV), BF),
            pltpu.VMEM((352, 448), BF),
            pltpu.VMEM((448, 416), BF),
            pltpu.VMEM((2, 4, NV, 256), BF),
            pltpu.VMEM((64, 64, 128), BF),
            pltpu.VMEM((8, 7, 64, 128), BF),
            pltpu.VMEM((8, 352, 128), BF),
            pltpu.VMEM((8, 416, 128), BF),
            pltpu.VMEM((8, 448, 128), BF),
            pltpu.VMEM((8, 448, 128), BF),
            pltpu.VMEM((8, 256, 512), BF),
            pltpu.VMEM((2, 256, 128), F32),
            pltpu.VMEM((16, 32, 128), F32),
            pltpu.VMEM((4, 8, 128), F32),
            pltpu.VMEM((16, 8, 128), F32),
            pltpu.VMEM((2, 4), jnp.int32),
            dma((3,)), dma((5,)), dma((5,)), dma((8, 7)), dma((8, 7)), dma((2, 8)), dma((2, 8)), dma((8,)), dma((8,)),
            dma((16,)), dma((16,)), dma((16,)), dma((16,)),
        ],
        compiler_params=pltpu.CompilerParams(
            collective_id=0, has_side_effects=True, vmem_limit_bytes=127 * 512 * 1024
        ),
        cost_estimate=pl.CostEstimate(flops=4 * 10**9, bytes_accessed=2 * 10**7, transcendentals=0),
        name="ladder_sum",
    )(amplitudes, integrals, pair_list.T)


def body(amplitudes, integrals, pair_list):
    return ladder_sum(amplitudes, integrals, pair_list).astype(BF)


def solution(mesh):
    placed = (P("pair", "slab"), P("pair", "slab"), P("slab", None))
    return jax.shard_map(
        body, mesh=mesh, in_specs=placed, out_specs=P("slab", "pair"), check_vma=False
    )
```

time: 98.8 us -> 87.9 us (0.89)
  the two profiles are of different devices: /device:TPU:15 before, /device:TPU:1 now
where the time goes in v3:
time: 87.9 us; the launch traced here: 87.7 us
  Pallas kernels  86.5 us (98%)
  other arithmetic  1.25 us (1%)
    pallas_call x1, Pallas kernels, ladder_sum(): pl.pallas_call(kernel, out_shape=jax.ShapeDtypeStruct((4, 64), F32), in_s...  86.5 us

profile of v3, /device:TPU:1, one launch (start us, length us, event | category | flops | bytes accessed | tf_op | source)
XLA Modules:
  0.0 87.7 jit_solution(13314724955828073059)
XLA Ops:
  0.0 86.5 %ladder_sum.1 = f32[4,64]{1,0:T(4,128)} custom-call(bf16[128,6272]{1,0:T(8,128)(2,1)} %amp.1, bf16[64,6272]{1,0:T(8,128)(2,1)} %ints.1, s32[2,4]{1,0:T(2,128)} %bitcast.1), custom_call_target="tpu_custom_call" | custom-call | flops 4000000000 | bytes 20000000 | tf_op jit(solution)/shard_map/ladder_sum/pallas_call | solution.py:411
  86.5 1.2 %convert_element_type.3 = bf16[4,64]{1,0:T(4,128)(2,1)} convert(f32[4,64]{1,0:T(4,128)} %ladder_sum.1) | non-fusion elementwise | flops 256 | bytes 1536 | tf_op jit(solution)/shard_map/convert_element_type | solution.py:447

commit v4 on v3

--- a/solution.py
+++ b/solution.py
@@ -136,17 +136,12 @@
         xx, yy = near[n]
         return pltpu.make_async_remote_copy(
             src_ref=w.at[(goes_to(t) // 2) * 8 + xx * 2 + yy], dst_ref=xin.at[t, back[n]],
-            send_sem=xy_s.at[t, n], recv_sem=xy_r.at[t, back[n]],
+            send_sem=xy_s.at[0], recv_sem=xy_r.at[t],
             device_id=(q, slab(xx, z, yy)), device_id_type=MESH,
         )
 
-    def xy_arrival(t, n):
-        xx, yy = near[n]
-        return pltpu.make_async_remote_copy(
-            src_ref=xin.at[t, n], dst_ref=xin.at[t, n],
-            send_sem=xy_s.at[t, n], recv_sem=xy_r.at[t, n],
-            device_id=(q, slab(xx, z, yy)), device_id_type=MESH,
-        )
+    def arrived(ref, sem):
+        pltpu.make_async_copy(ref, ref, sem).wait()
 
     def send_xy(t, carry):
         t = entry(SEND, t)
@@ -158,13 +153,13 @@
     def own_copy(t):
         return pltpu.make_async_remote_copy(
             src_ref=w.at[(goes_to(t) // 2) * 8 + me], dst_ref=zin.at[t, pl.ds(0, 64)],
-            send_sem=z_s.at[0, t], recv_sem=z_r.at[0, t], device_id=z_peer(t), device_id_type=MESH,
+            send_sem=z_s.at[0], recv_sem=z_r.at[0, t], device_id=z_peer(t), device_id_type=MESH,
         )
 
     def z_copy(t):
         return pltpu.make_async_remote_copy(
             src_ref=zout.at[t], dst_ref=zin.at[t, pl.ds(64, 352)],
-            send_sem=z_s.at[1, t], recv_sem=z_r.at[1, t], device_id=z_peer(t), device_id_type=MESH,
+            send_sem=z_s.at[1], recv_sem=z_r.at[1, t], device_id=z_peer(t), device_id_type=MESH,
         )
 
     def send_own(t, carry):
@@ -193,8 +188,7 @@
 
     def relay(t, carry):
         t = entry(SEND, t)
-        for n in range(7):
-            xy_arrival(t, n).wait_recv()
+        arrived(xin.at[t], xy_r.at[t])
         packed = dot(pack[...], xin[t].reshape(448, 128)).astype(BF)
         stays = offset(t) == 0
 
@@ -247,7 +241,7 @@
 
     def lo_copy(t):
         return pltpu.make_async_remote_copy(
-            src_ref=sym.at[t], dst_ref=other.at[t], send_sem=lo_s.at[t], recv_sem=lo_r.at[t],
+            src_ref=sym.at[t], dst_ref=other.at[t], send_sem=lo_s.at[0], recv_sem=lo_r.at[t],
             device_id=across, device_id_type=MESH,
         )
 
@@ -277,7 +271,6 @@
         return carry
 
     lax.fori_loop(0, 8, symmetrize, 0)
-    add_other(TAKE[7])
 
     mine16 = k * 8 + me
 
@@ -286,14 +279,7 @@
         side = jnp.where(yy == l, 0, 1)
         return pltpu.make_async_remote_copy(
             src_ref=acc.at[side, pl.ds(pl.multiple_of(kk * 128 + xx * 32, 32), 32)], dst_ref=r1in.at[mine16],
-            send_sem=r1_s.at[n], recv_sem=r1_r.at[mine16],
-            device_id=(l * 2 + kk, slab(xx, z, yy)), device_id_type=MESH,
-        )
-
-    def r1_arrival(n):
-        kk, xx, yy = n // 8, (n // 2) % 4, n % 2
-        return pltpu.make_async_remote_copy(
-            src_ref=r1in.at[n], dst_ref=r1in.at[n], send_sem=r1_s.at[n], recv_sem=r1_r.at[n],
+            send_sem=r1_s.at[0], recv_sem=r1_r.at[0],
             device_id=(l * 2 + kk, slab(xx, z, yy)), device_id_type=MESH,
         )
 
@@ -304,36 +290,29 @@
 
         return carry
 
-    lax.fori_loop(0, 16, r1_send, 0)
+    lax.fori_loop(0, 8, lambda i, carry: r1_send(2 * i + l, carry), 0)
+    add_other(TAKE[7])
+    lax.fori_loop(0, 8, lambda i, carry: r1_send(2 * i + 1 - l, carry), 0)
     total = acc[jnp.where(y == l, 0, 1), pl.ds(pl.multiple_of(k * 128 + x * 32, 32), 32)]
     r1in[mine16] = total
 
     for a in range(4):
         swap(part(k, a), a).wait_send()
     swap(a_all.at[k], 4).wait_send()
-
-    def drain(t, carry):
-        for n in range(7):
-            xy_copy(t, n).wait_send()
-
-        @pl.when(offset(t) != 0)
-        def _():
-            own_copy(t).wait_send()
-            z_copy(t).wait_send()
-
-        lo_copy(t).wait_send()
-        return carry
-
-    lax.fori_loop(0, 8, drain, 0)
-
-    def r1_wait(n, carry):
-        @pl.when(n != mine16)
-        def _():
-            r1_arrival(n).wait_recv()
-
-        return carry
-
-    lax.fori_loop(0, 16, r1_wait, 0)
+    arrived(w.at[pl.ds(0, 56)], xy_s.at[0])
+    arrived(sym, lo_s.at[0])
+
+    @pl.when(parity == 1)
+    def _():
+        arrived(w.at[pl.ds(0, 8)], z_s.at[0])
+        arrived(zout, z_s.at[1])
+
+    @pl.when(parity == 0)
+    def _():
+        arrived(w.at[pl.ds(0, 7)], z_s.at[0])
+        arrived(zout.at[pl.ds(0, 7)], z_s.at[1])
+
+    arrived(r1in.at[pl.ds(0, 15)], r1_r.at[0])
     r1sum[...] = jnp.sum(r1in[...], axis=0).reshape(4, 8, 128)
 
     def r2_owner(n):
@@ -343,7 +322,7 @@
     def r2_copy(n):
         qq, ss = r2_owner(n)
         return pltpu.make_async_remote_copy(
-            src_ref=r1sum.at[n // 4], dst_ref=r2in.at[z], send_sem=r2_s.at[n], recv_sem=r2_r.at[z],
+            src_ref=r1sum.at[n // 4], dst_ref=r2in.at[z], send_sem=r2_s.at[0], recv_sem=r2_r.at[0],
             device_id=(qq, ss), device_id_type=MESH,
         )
 
@@ -364,28 +343,21 @@
 
     lax.fori_loop(0, 16, r2_send, 0)
 
-    def drain_sums(n, carry):
-        @pl.when(n != mine16)
-        def _():
-            r1_copy(n).wait_send()
-
-        return carry
-
-    lax.fori_loop(0, 16, drain_sums, 0)
-
-    def r2_wait(n, carry):
-        qq, ss = x, slab(z // 4, n, q // 2)
-
-        @pl.when(jnp.logical_not((qq == q) & (ss == s)))
-        def _():
-            pltpu.make_async_remote_copy(
-                src_ref=r2in.at[n], dst_ref=r2in.at[n], send_sem=r2_s.at[n], recv_sem=r2_r.at[n],
-                device_id=(qq, ss), device_id_type=MESH,
-            ).wait_recv()
-
-        return carry
-
-    lax.fori_loop(0, 16, r2_wait, 0)
+    arrived(r1in.at[pl.ds(0, 15)], r1_s.at[0])
+
+    takes_own = (x == q) & (z // 4 == x) & (q // 2 == y)
+
+    def tiles(sem):
+        @pl.when(takes_own)
+        def _():
+            arrived(r2in.at[pl.ds(0, 15)], sem)
+
+        @pl.when(jnp.logical_not(takes_own))
+        def _():
+            arrived(r2in, sem)
+
+    tiles(r2_r.at[0])
+
     done = jnp.sum(r2in[...], axis=0)
     done = jnp.where(y == 0, done[:4], done[4:])
     done = jnp.where(k == 0, done[:, :64], done[:, 64:])
@@ -394,16 +366,7 @@
     weight = jnp.sum(jnp.where(r == c, weight, 0.0), axis=1, keepdims=True)
     out[...] = done * weight
 
-    def drain_tiles(n, carry):
-        qq, ss = r2_owner(n)
-
-        @pl.when(jnp.logical_not((qq == q) & (ss == s)))
-        def _():
-            r2_copy(n).wait_send()
-
-        return carry
-
-    lax.fori_loop(0, 16, drain_tiles, 0)
+    tiles(r2_s.at[0])
 
 
 def ladder_sum(amplitudes, integrals, pair_list):
@@ -432,8 +395,8 @@
             pltpu.VMEM((4, 8, 128), F32),
             pltpu.VMEM((16, 8, 128), F32),
             pltpu.VMEM((2, 4), jnp.int32),
-            dma((3,)), dma((5,)), dma((5,)), dma((8, 7)), dma((8, 7)), dma((2, 8)), dma((2, 8)), dma((8,)), dma((8,)),
-            dma((16,)), dma((16,)), dma((16,)), dma((16,)),
+            dma((3,)), dma((5,)), dma((5,)), dma((1,)), dma((8,)), dma((2,)), dma((2, 8)), dma((1,)), dma((8,)),
+            dma((1,)), dma((1,)), dma((1,)), dma((1,)),
         ],
         compiler_params=pltpu.CompilerParams(
             collective_id=0, has_side_effects=True, vmem_limit_bytes=127 * 512 * 1024

time: 87.9 us -> 85.1 us (0.968)
  the two profiles are of different devices: /device:TPU:1 before, /device:TPU:8 now
where the time goes in v4:
time: 85.1 us; the launch traced here: 84.6 us
  Pallas kernels  83.3 us (98%)
  other arithmetic  1.25 us (1%)
    pallas_call x1, Pallas kernels, ladder_sum(): pl.pallas_call(kernel, out_shape=jax.ShapeDtypeStruct((4, 64), F32), in_s...  83.3 us

profile of v4, /device:TPU:8, one launch (start us, length us, event | category | flops | bytes accessed | tf_op | source)
XLA Modules:
  0.0 84.6 jit_solution(881597394095155797)
XLA Ops:
  0.0 83.3 %ladder_sum.1 = f32[4,64]{1,0:T(4,128)} custom-call(bf16[128,6272]{1,0:T(8,128)(2,1)} %amp.1, bf16[64,6272]{1,0:T(8,128)(2,1)} %ints.1, s32[2,4]{1,0:T(2,128)} %bitcast.1), custom_call_target="tpu_custom_call" | custom-call | flops 4000000000 | bytes 20000000 | tf_op jit(solution)/shard_map/ladder_sum/pallas_call | solution.py:374
  83.3 1.2 %convert_element_type.3 = bf16[4,64]{1,0:T(4,128)(2,1)} convert(f32[4,64]{1,0:T(4,128)} %ladder_sum.1) | non-fusion elementwise | flops 256 | bytes 1536 | tf_op jit(solution)/shard_map/convert_element_type | solution.py:410

commit v5 on v4

--- a/solution.py
+++ b/solution.py
@@ -162,6 +162,12 @@
             send_sem=z_s.at[1], recv_sem=z_r.at[1, t], device_id=z_peer(t), device_id_type=MESH,
         )
 
+    def z_half(t, h):
+        return pltpu.make_async_remote_copy(
+            src_ref=zout.at[t, pl.ds(176 * h, 176)], dst_ref=zin.at[t, pl.ds(64 + 176 * h, 176)],
+            send_sem=z_s.at[1], recv_sem=z_r.at[1, t], device_id=z_peer(t), device_id_type=MESH,
+        )
+
     def send_own(t, carry):
         t = entry(SEND, t)
         stays = offset(t) == 0
@@ -199,7 +205,8 @@
         @pl.when(jnp.logical_not(stays))
         def _():
             zout[t] = packed
-            z_copy(t).start()
+            for h in range(2):
+                z_half(t, h).start()
 
         return carry
 

time: 85.1 us -> 85.1 us (level)
  the two profiles are of different devices: /device:TPU:8 before, /device:TPU:5 now
where the time goes in v5:
time: 85.1 us; the launch traced here: 84.9 us
  Pallas kernels  83.7 us (98%)
  other arithmetic  1.25 us (1%)
    pallas_call x1, Pallas kernels, ladder_sum(): pl.pallas_call(kernel, out_shape=jax.ShapeDtypeStruct((4, 64), F32), in_s...  83.7 us

profile of v5, /device:TPU:5, one launch (start us, length us, event | category | flops | bytes accessed | tf_op | source)
XLA Modules:
  0.0 84.9 jit_solution(3775655981158295219)
XLA Ops:
  0.0 83.7 %ladder_sum.1 = f32[4,64]{1,0:T(4,128)} custom-call(bf16[128,6272]{1,0:T(8,128)(2,1)} %amp.1, bf16[64,6272]{1,0:T(8,128)(2,1)} %ints.1, s32[2,4]{1,0:T(2,128)} %bitcast.1), custom_call_target="tpu_custom_call" | custom-call | flops 4000000000 | bytes 20000000 | tf_op jit(solution)/shard_map/ladder_sum/pallas_call | solution.py:381
  83.7 1.2 %convert_element_type.3 = bf16[4,64]{1,0:T(4,128)(2,1)} convert(f32[4,64]{1,0:T(4,128)} %ladder_sum.1) | non-fusion elementwise | flops 256 | bytes 1536 | tf_op jit(solution)/shard_map/convert_element_type | solution.py:417
